TPU v7x, 256 devices: a whole 4x4x8 slice. The times are simulated.
256 devices in a mesh: fsdp: 16 (over z, y_lo), dom: 16 (over y_hi, x, core).
Axes of the slice: x: 4, y: 4 (y_hi: 2, y_lo: 2; y = y_hi * 2 + y_lo), z: 8, core: 2. Of those that a mesh axis runs over, the one named last changes fastest.
Arguments:
- tokens: bfloat16 [65536, 8192], P(('fsdp', 'dom')), may hold values from -24 to 24
- key_grad: bfloat16 [65536, 512], P(('fsdp', 'dom')), may hold values from -6 to 6
- weight: bfloat16 [8192, 512], P('fsdp'), may hold values from -0.0625 to 0.0625
- master: float32 [8192, 512], P(('fsdp', 'dom')), may hold values from -0.0625 to 0.0625
- moment_one: float32 [8192, 512], P(('fsdp', 'dom')), may hold values from -3 to 3
- moment_two: float32 [8192, 512], P(('fsdp', 'dom')), may hold values from 0.1 to 4
- live: int32 [16, 16], replicated, may hold values from 0 to 1, as said below
- buddy: int32 [16], replicated, may hold values from 0 to 15, as said below
Outputs:
- keys: bfloat16 [65536, 512], P(('fsdp', 'dom'))
- input_grad: bfloat16 [65536, 8192], P(('fsdp', 'dom'))
- new_weight: bfloat16 [8192, 512], P('fsdp')
- new_master: float32 [8192, 512], P(('fsdp', 'dom'))
- new_one: float32 [8192, 512], P(('fsdp', 'dom'))
- new_two: float32 [8192, 512], P(('fsdp', 'dom'))
- held_copy: float32 [3, 8192, 512], P(None, ('fsdp', 'dom'))
Inputs may be any that keep to these rules, and one draw needn't show every extreme that they name: `live`: every column (domain) has at least one 1. A permutation of the domains in a single cycle; no domain is its own buddy; some domain's buddy lies 16 / 2 domains further round.
All inputs are finite; a program needn't handle non-finite values.
Results may differ from a plain program's by a relative error of at most 0.005.
Values may be sent and summed in bfloat16 or wider, within the bound.
A program may use at most 128 MiB of HBM per device.

v0:
```python
import jax
import jax.numpy as jnp
from jax import lax
from jax.sharding import PartitionSpec as P

STEP = 100


def on_device(tokens, key_grad, weight, master, moment_one, moment_two, live, buddy):
    domains = lax.axis_size("dom")
    member = lax.axis_index("fsdp")
    domain = lax.axis_index("dom")
    xf = tokens.astype(jnp.float32)
    rstd = lax.rsqrt(jnp.mean(xf * xf, axis=1, keepdims=True) + 1e-05)
    hat = xf * rstd
    normed = hat.astype(jnp.bfloat16)
    contract = (((1,), (1,)), ((), ()))
    whole = lax.all_gather(weight, "fsdp", axis=0, tiled=True)
    keys = jnp.dot(normed, whole, preferred_element_type=jnp.float32)
    back = lax.dot_general(key_grad, whole, contract, preferred_element_type=jnp.float32)
    keys = keys.astype(jnp.bfloat16)
    input_grad = (rstd * (back - hat * jnp.mean(back * hat, axis=1, keepdims=True))).astype(
        jnp.bfloat16
    )
    live_float = live.astype(jnp.float32)
    norming = live.shape[0] * live.shape[1] / (jnp.sum(live_float) * tokens.shape[0])
    alive_here = lax.dynamic_index_in_dim(
        lax.dynamic_index_in_dim(live_float, member, 0, keepdims=False), domain, 0, keepdims=False
    )
    scale = alive_here * norming
    product = lax.dot_general(
        normed, key_grad, (((0,), (0,)), ((), ())), preferred_element_type=jnp.float32
    )
    group_part = lax.psum_scatter(product * scale, "fsdp", scatter_dimension=0, tiled=True)
    grad = lax.psum_scatter(group_part, "dom", scatter_dimension=0, tiled=True)
    new_one = 0.9 * moment_one + 0.1 * grad
    new_two = 0.95 * moment_two + 0.05 * grad * grad
    first = 1.0 - 0.9**STEP
    second = 1.0 - 0.95**STEP
    update = new_one / first / (jnp.sqrt(new_two / second) + 1e-08)
    new_master = master - 0.002 * (update + 0.1 * master)
    new_weight = lax.all_gather(new_master.astype(jnp.bfloat16), "dom", axis=0, tiled=True)
    state = jnp.stack((new_master, new_one, new_two))[None]
    slots = jnp.arange(domains, dtype=jnp.int32)
    source = jnp.sum(slots * (buddy == domain).astype(jnp.int32))
    everything = lax.all_gather(state, "dom", axis=0, tiled=True)
    held = lax.dynamic_index_in_dim(everything, source, 0, keepdims=False)
    return (keys, input_grad, new_weight, new_master, new_one, new_two, held)


def solution(mesh):
    placed = (
        P(("fsdp", "dom"), None),
        P(("fsdp", "dom"), None),
        P("fsdp", None),
        P(("fsdp", "dom"), None),
        P(("fsdp", "dom"), None),
        P(("fsdp", "dom"), None),
        P(),
        P(),
    )
    return jax.shard_map(
        on_device,
        mesh=mesh,
        in_specs=placed,
        out_specs=(
            P(("fsdp", "dom"), None),
            P(("fsdp", "dom"), None),
            P("fsdp", None),
            P(("fsdp", "dom"), None),
            P(("fsdp", "dom"), None),
            P(("fsdp", "dom"), None),
            P(None, ("fsdp", "dom"), None),
        ),
        check_vma=False,
    )
```

profile of v0, /device:TPU:97, one launch (start us, length us, event | category | flops | bytes accessed | tf_op | source)
XLA Modules:
  0.0 713.0 jit_solution(8398103320962988022)
XLA Ops:
  7.2 0.0 reduce-scatter.3.cloned.1.call-start
  7.2 0.7 convert_element_type.23
  8.0 1.3 convert_reduce_fusion
  10.0 3.1 fusion.7
  13.1 0.6 dynamic_slice.10
  14.3 10.4 %convolution_multiply_fusion = f32[8192,512]{1,0:T(8,128)} fusion(bf16[256,512]{1,0:T(8,128)(2,1)S(1)} %copy-done, f32[]{:T(128)S(6)} %mul.86, bf16[256,8192]{1,0:T(8,128)(2,1)} %param.8, f32[256]{0:T(256)S(1)} %add_rsqrt_fusion), kind=kOutput, calls=%fused_computation | convolution fusion | flops 2157969408 | bytes 21234692 | tf_op jit(solution)/shard_map/dot_general | solution.py:31
  24.8 0.0 reduce-scatter.3.cloned.1.call-update
  24.8 0.0 reduce-scatter.5.cloned.1.call-start
  24.8 353.7 %reduce-scatter.3.cloned.1.call-done = f32[512,512]{1,0:T(8,128)} async-done(((f32[8192,512]{1,0:T(8,128)}), f32[512,512]{1,0:T(8,128)}) %reduce-scatter.3.cloned.1.call-update) | async-done | bytes 1048592 | tf_op jit(solution)/shard_map/reduce_scatter | solution.py:34
  378.5 0.0 all-gather.4.cloned.1.call-start
  378.6 0.7 all-gather.4.cloned.1.call-update
  379.3 0.0 all-gather.6.cloned.1.call-start
  379.3 76.6 %reduce-scatter.5.cloned.1.call-done = f32[32,512]{1,0:T(8,128)} async-done(((f32[512,512]{1,0:T(8,128)}), f32[32,512]{1,0:T(8,128)}) %reduce-scatter.5.cloned.1.call-update) | async-done | bytes 65552 | tf_op jit(solution)/shard_map/reduce_scatter | solution.py:35
  455.9 0.9 fusion.16
  456.8 0.7 pad_maximum_fusion
  457.6 0.6 fusion.15
  460.2 181.4 %all-gather.4.cloned.1.call-done = bf16[8192,512]{1,0:T(8,128)(2,1)} async-done(((bf16[512,512]{1,0:T(8,128)(2,1)}), bf16[8192,512]{1,0:T(8,128)(2,1)}) %all-gather.4.cloned.1.call-update) | async-done | bytes 8388624 | tf_op jit(solution)/shard_map/all_gather | solution.py:18
  641.5 7.2 %fusion.3 = (f32[256]{0:T(256)S(1)}, f32[256,8192]{1,0:T(8,128)S(1)}) fusion(bf16[256,8192]{1,0:T(8,128)(2,1)} %param.8, f32[256]{0:T(256)S(1)} %add_rsqrt_fusion, bf16[256,512]{1,0:T(8,128)(2,1)S(1)} %copy-done, bf16[8192,512]{1,0:T(8,128)(2,1)} %all-gather.4.cloned.1.call-done), kind=kOutput, calls=%fused_computation.6 | convolution fusion | flops 2155872000 | bytes 21235712 | tf_op jit(solution)/shard_map/dot_general | solution.py:20
  648.8 6.4 fusion.11
  655.2 3.1 fusion.6
  658.3 25.9 %all_gather.10 = bf16[512,512]{1,0:T(8,128)(2,1)S(1)} all-gather(bf16[32,512]{1,0:T(8,128)(2,1)S(1)} %get-tuple-element.7), channel_id=1, replica_groups=mesh['fsdp'=16,'dom'=16] {'dom'}, dimensions={0}, use_global_device_ids=true | all-gather | bytes 557056 | tf_op jit(solution)/shard_map/all_gather | solution.py:42
  684.2 19.8 %all-gather.6.cloned.1.call-done = f32[48,32,512]{2,1,0:T(8,128)} async-done(((f32[3,32,512]{2,1,0:T(8,128)}), f32[48,32,512]{2,1,0:T(8,128)}) %all-gather.6.cloned.1.call-update) | async-done | bytes 3145744 | tf_op jit(solution)/shard_map/all_gather | solution.py:46
  704.0 1.6 dynamic-slice_bitcast_fusion
  705.7 0.8 copy.16
  (22 shorter events, 0.1 us)
Async XLA Ops:
  7.2 7.2 %copy-start = (bf16[256,512]{1,0:T(8,128)(2,1)S(1)}, bf16[256,512]{1,0:T(8,128)(2,1)}, u32[]{:S(2)}) copy-start(bf16[256,512]{1,0:T(8,128)(2,1)} %param.9) | copy-start | bytes 786436
  7.2 371.3 %reduce-scatter.3.cloned.1.call-start = ((), (), s32[]{:S(2)}) async-start(), calls=%async_computation.3 | async-start | bytes 17825792 | tf_op jit(solution)/shard_map/reduce_scatter | solution.py:34
  24.8 431.1 %copy-start.5 = (f32[32,512]{1,0:T(8,128)S(1)}, f32[32,512]{1,0:T(8,128)}, u32[]{:S(2)}) copy-start(f32[32,512]{1,0:T(8,128)} %param.11) | copy-start | bytes 196612
  24.8 431.1 %copy-start.6 = (f32[32,512]{1,0:T(8,128)S(1)}, f32[32,512]{1,0:T(8,128)}, u32[]{:S(2)}) copy-start(f32[32,512]{1,0:T(8,128)} %param.12) | copy-start | bytes 196612
  24.8 431.1 %copy-start.7 = (f32[32,512]{1,0:T(8,128)S(1)}, f32[32,512]{1,0:T(8,128)}, u32[]{:S(2)}) copy-start(f32[32,512]{1,0:T(8,128)} %param.13) | copy-start | bytes 196612
  24.8 432.8 %copy-start.8 = (s32[16]{0:T(128)S(1)}, s32[16]{0:T(128)}, u32[]{:S(2)}) copy-start(s32[16]{0:T(128)} %param.15) | copy-start | bytes 196
  24.8 431.1 %reduce-scatter.5.cloned.1.call-start = ((), (), s32[]{:S(2)}) async-start(), calls=%async_computation.4 | async-start | bytes 1114112 | tf_op jit(solution)/shard_map/reduce_scatter | solution.py:35
  378.5 263.0 %all-gather.4.cloned.1.call-start = ((), (), s32[]{:S(2)}) async-start(), calls=%async_computation.2 | async-start | bytes 8912896 | tf_op jit(solution)/shard_map/all_gather | solution.py:18
  379.3 324.8 %all-gather.6.cloned.1.call-start = ((), (), s32[]{:S(2)}) async-start(), calls=%async_computation.5 | async-start | bytes 3342336 | tf_op jit(solution)/shard_map/all_gather | solution.py:46
  456.8 191.9 %copy-start.2 = (f32[32,512]{1,0:T(8,128)}, f32[32,512]{1,0:T(8,128)S(1)}, u32[]{:S(2)}) copy-start(f32[32,512]{1,0:T(8,128)S(1)} %get-tuple-element.23) | copy-start | bytes 196612
  456.8 191.9 %copy-start.3 = (f32[32,512]{1,0:T(8,128)}, f32[32,512]{1,0:T(8,128)S(1)}, u32[]{:S(2)}) copy-start(f32[32,512]{1,0:T(8,128)S(1)} %get-tuple-element.24) | copy-start | bytes 196612
  456.8 191.9 %copy-start.4 = (f32[32,512]{1,0:T(8,128)}, f32[32,512]{1,0:T(8,128)S(1)}, u32[]{:S(2)}) copy-start(f32[32,512]{1,0:T(8,128)S(1)} %get-tuple-element.25) | copy-start | bytes 196612
  641.5 7.2 %copy-start.1 = (bf16[256,8192]{1,0:T(8,128)(2,1)S(1)}, bf16[256,8192]{1,0:T(8,128)(2,1)}, u32[]{:S(2)}) copy-start(bf16[256,8192]{1,0:T(8,128)(2,1)} %param.8) | copy-start | bytes 12582916
Sparse Core Ops, SparseCore 0:
  24.9 353.5 reduce-scatter.2
  382.6 73.2 reduce-scatter.4
  457.8 183.6 all-gather.3
  645.1 58.9 all-gather.5
where the time goes:
time: 715 us; the launch traced here: 713 us
  waiting for transfers between devices  632 us (88%)
  blocking collectives  25.9 us (4%)
  matrix products  24.1 us (3%)
  between operations  17.2 us (2%)
  other arithmetic  10.5 us (1%)
    reduce_scatter x1, waiting for transfers between devices, on_device(): lax.psum_scatter(product * scale, 'fsdp', scatter_dimension=0, tiled=True)  354 us
    all_gather x1, waiting for transfers between devices, on_device(): whole = lax.all_gather(weight, 'fsdp', axis=0, tiled=True)  181 us
    reduce_scatter x1, waiting for transfers between devices, on_device(): grad = lax.psum_scatter(group_part, 'dom', scatter_dimension=0, tiled=True)  76.6 us
    all_gather x1, blocking collectives, on_device(): lax.all_gather(new_master.astype(jnp.bfloat16), 'dom', axis=0, tiled=True)  25.9 us
    all_gather x1, waiting for transfers between devices, on_device(): everything = lax.all_gather(state, 'dom', axis=0, tiled=True)  19.8 us
  transfers between devices with their start and end apart: 4, of which 4 were waited for; matrix products, arithmetic and copies ran while one was open for 3% of the time, Pallas kernels for 0%

commit v1 on v0

v1 whole, which is shorter than its diff:
```python
import functools

import jax
import jax.numpy as jnp
from jax import lax
from jax.experimental import pallas as pl
from jax.experimental.pallas import tpu as pltpu
from jax.sharding import PartitionSpec as P

STEP = 100
F32 = jnp.float32
BF16 = jnp.bfloat16
MESH = pl.DeviceIdType.MESH
ORDER = (
    "send0", "prod0", "prod1", "pair0", "prod2", "pair1", "ag1", "prod3", "xb0", "pair2",
    "agy0", "comp0", "y0", "ag2", "agy1", "xb1", "pair3", "z0", "comp1", "y1", "ag3", "agy2",
    "xb2", "z1", "comp2", "y2", "ag4", "agy3", "xb3", "z2", "y3", "z3", "update", "agy4",
    "comp3", "comp4", "final", "spread",
)


def dot(a, b, ca, cb):
    return lax.dot_general(a, b, (((ca,), (cb,)), ((), ())), preferred_element_type=F32)


def kernel(
    tok_h, kg_h, w_h, ma_h, mo_h, mt_h, live_v, buddy_s,
    keys_h, ig_h, nw_h, nm_h, n1_h, n2_h, held_h,
    tok, kg, kgm, W, back, keysf, keysb, normed, rstd, dots, prod, R, XA, XB, YS, YR, ZS, ZR, Zown, GA,
    state, new, held,
    loc, pair_s, pair_r, xa_s, xa_r, xb_s, xb_r, ys_s, ys_r, zs_s, zs_r,
    az_s, az_r, ay_s, ay_r, sib_s, sib_r, ga_s, ga_r, gs_s, gs_r,
):
    f = lax.axis_index("fsdp")
    d = lax.axis_index("dom")
    z, ylo = lax.div(f, 2), lax.rem(f, 2)
    yhi, x, c = lax.div(d, 8), lax.rem(lax.div(d, 2), 4), lax.rem(d, 2)
    y = yhi * 2 + ylo
    o = 1 - c
    xp, xo, xm = lax.rem(x + 1, 4), lax.rem(x + 2, 4), lax.rem(x + 3, 4)

    def dev(x, y, z, c):
        return (z * 2 + lax.rem(y, 2), lax.div(y, 2) * 8 + x * 2 + c)

    def yat(j):
        return lax.rem(y + j, 4)

    def zat(j):
        return lax.rem(z + j, 8)

    sibling = dev(x, y, z, o)

    def local(i, src, dst):
        return pltpu.make_async_copy(src, dst, loc.at[i])

    def remote(src, dst, s, r, to):
        return pltpu.make_async_remote_copy(
            src_ref=src, dst_ref=dst, send_sem=s, recv_sem=r, device_id=to, device_id_type=MESH
        )

    loads = [
        local(0, w_h, W.at[f]),
        local(1, tok_h, tok),
        local(2, kg_h, kg),
        local(3, ma_h, state.at[0]),
        local(4, mo_h, state.at[1]),
        local(5, mt_h, state.at[2]),
    ]
    for copy in loads:
        copy.start()

    barrier = pltpu.get_barrier_semaphore()
    partners = [sibling]
    partners += [dev(lax.rem(x + i, 4), y, z, c) for i in (1, 2, 3)]
    partners += [dev(lax.rem(x + i, 4), yat(2), z, c) for i in (0, 1, 2, 3)]
    partners += [dev(x, yat(i), z, c) for i in (1, 3)]
    partners += [dev(x, y, zat(i), c) for i in range(1, 8)]
    for who in partners:
        pl.semaphore_signal(barrier, inc=1, device_id=who, device_id_type=MESH)
    pl.semaphore_wait(barrier, len(partners))

    def z_offset(k, core):
        one = 1 - 2 * core
        return -one * k if k <= 4 else one * (k - 4)

    def piece(k, core, other):
        zz = lax.rem(z + z_offset(k, core) + 8, 8)
        return zz * 2 + (1 - ylo if other else ylo)

    onward = dev(x, y, lax.rem(z + 1 - 2 * c + 8, 8), c)
    backward = dev(x, y, lax.rem(z - 1 + 2 * c + 8, 8), c)

    def az(k):
        to = onward if k < 5 else backward
        before = (k - 1) if k != 5 else 0
        src = W.at[piece(before, c, False), c]
        return remote(src, src, az_s.at[k - 1], az_r.at[k - 1], to)

    def az_in(k):
        src = W.at[piece(k, c, False), c]
        return remote(src, src, az_s.at[k - 1], az_r.at[k - 1], onward)

    def ay(k, side):
        src = W.at[piece(k, c, False), c, side]
        return remote(src, src, ay_s.at[k, side], ay_r.at[k, side], dev(x, yat(1 if side == 0 else 3), z, c))

    def ay_in(k, side):
        src = W.at[piece(k, c, True), c, side]
        return remote(src, src, ay_s.at[k, side], ay_r.at[k, side], dev(x, yat(1), z, c))

    def sib(k, other):
        src = W.at[piece(k, c, other), c]
        i = k + 8 * other
        return remote(src, src, sib_s.at[i], sib_r.at[i], sibling)

    def sib_in(k, other):
        src = W.at[piece(k, o, other), o]
        i = k + 8 * other
        return remote(src, src, sib_s.at[i], sib_r.at[i], sibling)

    sent = []

    def go(copy):
        copy.start()
        sent.append(copy)

    steps = {0: (0,), 1: (1, 5), 2: (2, 6), 3: (3, 7), 4: (4,)}

    def gather(s):
        for k in steps[s]:
            if s:
                az_in(k).wait_recv()
            if k == 0:
                go(az(1))
                go(az(5))
            elif k not in (4, 7):
                go(az(k + 1))
            go(ay(k, 0))
            go(ay(k, 1))
            if k:
                go(sib(k, False))

    def gather_y(s):
        for k in steps[s]:
            ay_in(k, 0).wait_recv()
            ay_in(k, 1).wait_recv()
            go(sib(k, True))

    def send0():
        loads[0].wait()
        gather(0)
        loads[1].wait()
        dots[...] = jnp.zeros_like(dots)

        @pl.loop(0, 16)
        def _(i):
            v = tok[:, pl.ds(pl.multiple_of(i * 512, 512), 512)].astype(F32)
            v = v * v
            dots[...] += (v[:, :128] + v[:, 128:256]) + (v[:, 256:384] + v[:, 384:])

        mean = jnp.sum(dots[...], axis=1, keepdims=True) * (1.0 / 8192)
        rstd[...] = jnp.broadcast_to(lax.rsqrt(mean + 1e-05), rstd.shape)
        dots[...] = jnp.zeros_like(dots)
        keysf[...] = jnp.zeros_like(keysf)
        live = live_v[...].astype(F32)
        rows = lax.broadcasted_iota(jnp.int32, live.shape, 0)
        cols = lax.broadcasted_iota(jnp.int32, live.shape, 1)
        alive = jnp.sum(jnp.where((rows == f) & (cols == d), live, 0.0))
        loads[2].wait()
        kgm[...] = (kg[...].astype(F32) * alive).astype(BF16)

    def wide(column):
        return jnp.concatenate([column] * 4, axis=1)

    def product(g):
        @pl.loop(0, 4)
        def _(fi):
            at = pl.ds(pl.multiple_of((g * 4 + fi) * 512, 512), 512)
            normed[:, at] = (tok[:, at].astype(F32) * wide(rstd[...])).astype(BF16)
            part = dot(normed[:, at], kgm[...], 0, 0).astype(BF16)
            for yy in range(2):
                for xx in range(4):
                    for cc in range(2):
                        row = yy * 256 + xx * 64 + cc * 32
                        prod[g, cc, xx, yy, fi] = part[row : row + 32]

        go(pair(g))

    def pair(g):
        return remote(prod.at[g, o], R.at[g], pair_s.at[g], pair_r.at[g], sibling)

    def xa(g, i):
        block, half, to = ((xo, 0, xp), (xp, 1, xp), (xo, 1, xm), (xm, 0, xm))[i]
        return remote(
            prod.at[g, c, block, half], XA.at[g, i], xa_s.at[g, i], xa_r.at[g, i], dev(to, y, z, c)
        )

    def xb(g, i):
        block = (xp, xm)[i]
        return remote(
            prod.at[g, c, block, i], XB.at[g, i], xb_s.at[g, i], xb_r.at[g, i], dev(block, y, z, c)
        )

    def ysend(g, j):
        return remote(
            YS.at[g, yat(j)], YR.at[g, j - 1], ys_s.at[g, j - 1], ys_r.at[g, j - 1], dev(x, yat(j), z, c)
        )

    def pair_sum(g):
        pair(g).wait_recv()

        @pl.loop(0, 8)
        def _(i):
            xx, yy = lax.div(i, 2), lax.rem(i, 2)
            for fi in range(4):
                prod[g, c, xx, yy, fi] = (
                    prod[g, c, xx, yy, fi].astype(F32) + R[g, xx, yy, fi].astype(F32)
                ).astype(BF16)

        for i in (0, 2, 1, 3):
            go(xa(g, i))

    def x_second(g):
        for i, block in ((0, xp), (1, xm)):
            xa(g, 2 * i).wait_recv()

            @pl.loop(0, 4)
            def _(fi):
                prod[g, c, block, i, fi] = (
                    prod[g, c, block, i, fi].astype(F32) + XA[g, 2 * i, fi].astype(F32)
                ).astype(BF16)

            go(xb(g, i))

    def y_stage(g):
        for half, i in ((0, 3), (1, 1)):
            xa(g, i).wait_recv()
            xb(g, half).wait_recv()

            @pl.loop(0, 4)
            def _(fi):
                total = prod[g, c, x, half, fi].astype(F32) + XA[g, i, fi].astype(F32)
                total = total + XB[g, half, fi].astype(F32)
                YS[g, half * 2 + lax.rem(fi, 2), lax.div(fi, 2)] = total.astype(BF16)

        for j in (2, 1, 3):
            go(ysend(g, j))

    def zsend(g, i):
        return remote(
            ZS.at[g, i], ZR.at[z], zs_s.at[g, i], zs_r.at[z], dev(x, y, 2 * g + i, c)
        )

    def z_stage(g):
        for j in (1, 2, 3):
            ysend(g, j).wait_recv()
        for i in range(2):
            total = YS[g, y, i].astype(F32)
            for j in range(3):
                total = total + YR[g, j, i].astype(F32)

            @pl.when(z == 2 * g + i)
            def _():
                Zown[...] = total

            @pl.when(z != 2 * g + i)
            def _():
                ZS[g, i] = total.astype(BF16)
                zsend(g, i).start()

    chip = lax.div(d, 2)
    others = [(i, j) for j in (0, 2) for i in range(4) if i or j]

    def spread_out(n):
        i, j = others[n]
        to = dev(lax.rem(x + i, 4), yat(j), z, c)
        return remote(GA.at[c, chip], GA.at[c, chip], ga_s.at[n], ga_r.at[n], to)

    def spread_in(n):
        i, j = others[n]
        xx, yy = lax.rem(x - i + 4, 4), yat(j)
        slot = GA.at[c, lax.div(yy, 2) * 4 + xx]
        return remote(slot, slot, ga_s.at[n], ga_r.at[n], sibling)

    def spread_pair():
        return remote(GA.at[c], GA.at[c], gs_s.at[0], gs_r.at[0], sibling)

    def spread_pair_in():
        return remote(GA.at[o], GA.at[o], gs_s.at[0], gs_r.at[0], sibling)

    outs = [
        local(0, new.at[0], nm_h),
        local(1, new.at[1], n1_h),
        local(2, new.at[2], n2_h),
        local(3, held, held_h),
        local(4, GA.at[0, :, 0], nw_h.at[:, 0]),
        local(5, GA.at[1, :, 0], nw_h.at[:, 1]),
        local(6, keysb, keys_h),
    ]

    def ig_out(i):
        at = pl.ds(pl.multiple_of(i * 1024, 1024), 1024)
        return pltpu.make_async_copy(tok.at[:, at], ig_h.at[:, at], loc.at[8 + i])

    def update():
        total = Zown[...]
        for j in range(1, 8):
            slot = zat(j)
            here = ZR.at[slot]
            remote(here, here, zs_s.at[0, 0], zs_r.at[slot], sibling).wait_recv()
            total = total + ZR[slot].astype(F32)
        live = live_v[...].astype(F32)
        grad = total * (256.0 / (jnp.sum(live) * 256.0))
        for copy in loads[3:]:
            copy.wait()
        one = 0.9 * state[1] + 0.1 * grad
        two = 0.95 * state[2] + 0.05 * grad * grad
        first = 1.0 - 0.9**STEP
        second = 1.0 - 0.95**STEP
        step = one / first / (jnp.sqrt(two / second) + 1e-08)
        master = state[0] - 0.002 * (step + 0.1 * state[0])
        for i, v in enumerate((master, one, two)):
            new[i] = v
            GA[c, chip, i] = v.astype(BF16)
        for n in range(7):
            go(spread_out(n))
        for copy in outs[:3]:
            copy.start()

    def spread():
        for n in range(7):
            spread_in(n).wait_recv()
        go(spread_pair())
        spread_pair_in().wait_recv()
        outs[4].start()
        outs[5].start()
        src = jnp.int32(0)
        for s in range(16):
            src = jnp.where(buddy_s[s] == d, s, src)
        held[...] = GA[lax.rem(src, 2), lax.div(src, 2)].astype(F32)
        outs[3].start()

    def compute(s):
        for k in steps[s]:
            mirror = 0 if s == 0 else 4 if s == 4 else k + 4 if k < 4 else k - 4
            for other in (False, True):
                if k or other:
                    sib_in(mirror, other).wait_recv()
                ff = piece(k, c, other)
                at = pl.ds(pl.multiple_of(ff * 512, 512), 512)
                w = W[ff].reshape(512, 512)
                keysf[...] += dot(normed[:, at], w, 1, 0)
                b = dot(kg[...], w, 1, 1)
                back[:, at] = b
                v = b * (tok[:, at].astype(F32) * wide(rstd[...]))
                dots[...] += (v[:, :128] + v[:, 128:256]) + (v[:, 256:384] + v[:, 384:])

    def final():
        keysb[...] = keysf[...].astype(BF16)
        outs[6].start()
        mean = jnp.sum(dots[...], axis=1, keepdims=True) * (1.0 / 8192)
        dots[...] = jnp.broadcast_to(mean, dots.shape)

        @pl.loop(0, 16)
        def _(i):
            at = pl.ds(pl.multiple_of(i * 512, 512), 512)
            r = wide(rstd[...])
            hat = tok[:, at].astype(F32) * r
            tok[:, at] = (r * (back[:, at] - hat * wide(dots[...]))).astype(BF16)

        for i in range(8):
            ig_out(i).start()

    run = dict(send0=send0, update=update, spread=spread, final=final)
    for s in range(5):
        run[f"ag{s}"] = functools.partial(gather, s)
        run[f"agy{s}"] = functools.partial(gather_y, s)
        run[f"comp{s}"] = functools.partial(compute, s)
    for g in range(4):
        run[f"prod{g}"] = functools.partial(product, g)
        run[f"pair{g}"] = functools.partial(pair_sum, g)
        run[f"xb{g}"] = functools.partial(x_second, g)
        run[f"y{g}"] = functools.partial(y_stage, g)
        run[f"z{g}"] = functools.partial(z_stage, g)
    for name in ORDER:
        run[name]()

    for copy in sent:
        copy.wait_send()
    for g in range(4):
        for i in range(2):

            @pl.when(z != 2 * g + i)
            def _():
                zsend(g, i).wait_send()

    for copy in outs:
        copy.wait()
    for i in range(8):
        ig_out(i).wait()


def on_device(tokens, key_grad, weight, master, moment_one, moment_two, live, buddy):
    hbm = pl.BlockSpec(memory_space=pl.ANY)
    dma = pltpu.SemaphoreType.DMA
    out = jax.ShapeDtypeStruct
    vm = pltpu.VMEM
    keys, ig, nw, nm, n1, n2, held = pl.pallas_call(
        kernel,
        out_shape=(
            out((256, 512), BF16),
            out((256, 8192), BF16),
            out((8, 2, 32, 512), BF16),
            out((32, 512), F32),
            out((32, 512), F32),
            out((32, 512), F32),
            out((3, 32, 512), F32),
        ),
        in_specs=[hbm] * 6
        + [pl.BlockSpec(memory_space=pltpu.VMEM), pl.BlockSpec(memory_space=pltpu.SMEM)],
        out_specs=(hbm,) * 7,
        scratch_shapes=[
            vm((256, 8192), BF16),
            vm((256, 512), BF16),
            vm((256, 512), BF16),
            vm((16, 2, 2, 128, 512), BF16),
            vm((256, 8192), F32),
            vm((256, 512), F32),
            vm((256, 512), BF16),
            vm((256, 8192), BF16),
            vm((256, 128), F32),
            vm((256, 128), F32),
            vm((4, 2, 4, 2, 4, 32, 512), BF16),
            vm((4, 4, 2, 4, 32, 512), BF16),
            vm((4, 4, 4, 32, 512), BF16),
            vm((4, 2, 4, 32, 512), BF16),
            vm((4, 4, 2, 32, 512), BF16),
            vm((4, 3, 2, 32, 512), BF16),
            vm((4, 2, 32, 512), BF16),
            vm((8, 32, 512), BF16),
            vm((32, 512), F32),
            vm((2, 8, 3, 32, 512), BF16),
            vm((3, 32, 512), F32),
            vm((3, 32, 512), F32),
            vm((3, 32, 512), F32),
            dma((16,)),
            dma((4,)), dma((4,)),
            dma((4, 4)), dma((4, 4)),
            dma((4, 2)), dma((4, 2)),
            dma((4, 3)), dma((4, 3)),
            dma((4, 2)), dma((8,)),
            dma((7,)), dma((7,)),
            dma((8, 2)), dma((8, 2)),
            dma((16,)), dma((16,)),
            dma((7,)), dma((7,)),
            dma((1,)), dma((1,)),
        ],
        compiler_params=pltpu.CompilerParams(
            collective_id=0, has_side_effects=True, vmem_limit_bytes=58 << 20
        ),
        cost_estimate=pl.CostEstimate(flops=6 << 30, bytes_accessed=24 << 20, transcendentals=0),
    )(tokens, key_grad, weight.reshape(2, 2, 128, 512), master, moment_one, moment_two, live, buddy)
    return keys, ig, nw.reshape(512, 512), nm, n1, n2, held


def solution(mesh):
    both = P(("fsdp", "dom"), None)
    return jax.shard_map(
        on_device,
        mesh=mesh,
        in_specs=(both, both, P("fsdp", None), both, both, both, P(), P()),
        out_specs=(both, both, P("fsdp", None), both, both, both, P(None, ("fsdp", "dom"), None)),
        check_vma=False,
    )
```

time: 715 us -> 91.5 us (0.13)
  the two profiles are of different devices: /device:TPU:97 before, /device:TPU:225 now
where the time goes in v1:
time: 91.5 us; the launch traced here: 91.3 us
  Pallas kernels  80.9 us (88%)
  local copies, waits for them, and re-layouts  9.76 us (11%)
    pallas_call x1, Pallas kernels, on_device(): pl.pallas_call(kernel, out_shape=(out((256, 512), BF16), out((256, 8192),...  80.9 us
    unnamed x17, local copies, waits for them, and re-layouts  9.76 us

profile of v1, /device:TPU:225, one launch (start us, length us, event | category | flops | bytes accessed | tf_op | source)
XLA Modules:
  0.0 91.3 jit_solution(12704247110547999992)
XLA Ops:
  0.6 80.9 %shard_map.135 = (bf16[256,512]{1,0:T(8,128)(2,1)}, bf16[256,8192]{1,0:T(8,128)(2,1)}, bf16[8,2,32,512]{3,2,1,0:T(8,128)(2,1)}, f32[32,512]{1,0:T(8,128)}, f32[3...) custom-call(bf16[256,8192]{1,0:T(8,128)(2,1)} %tok_h.1, bf16[256,512]{1,0:T(8,128)(2,1)} %kg_h.1, ...), custom_call_target="tpu_custom_call" | custom-call | flops 6442450944 | bytes 25165824 | tf_op jit(solution)/shard_map/pallas_call | solution.py:408
  81.5 1.7 %copy.22 = bf16[256,512]{1,0:T(8,128)(2,1)} copy(bf16[256,512]{1,0:T(8,128)(2,1)} %get-tuple-element.28) | data formatting | bytes 524288
  83.2 0.0 copy-start
  83.2 0.0 copy-start.4
  83.2 0.0 copy-start.3
  83.2 0.0 copy-start.2
  83.2 0.0 copy-start.1
  83.2 4.7 %copy.23 = bf16[256,8192]{1,0:T(8,128)(2,1)} copy(bf16[256,8192]{1,0:T(8,128)(2,1)} %get-tuple-element.29) | data formatting | bytes 8388608
  87.9 0.0 copy-done
  87.9 0.8 copy.24
  88.7 0.0 copy-done.4
  88.7 0.6 copy.25
  89.4 0.0 copy-done.3
  89.4 0.6 copy.26
  90.0 0.0 copy-done.2
  90.0 0.6 copy.27
  90.6 0.0 copy-done.1
  90.6 0.7 copy.28
Async XLA Ops:
  83.2 4.7 %copy-start = (bf16[8,2,32,512]{3,2,1,0:T(8,128)(2,1)S(1)}, bf16[8,2,32,512]{3,2,1,0:T(8,128)(2,1)}, u32[]{:S(2)}) copy-start(bf16[8,2,32,512]{3,2,1,0:T(8,128)(2,1)} %get-tuple-element.16) | copy-start | bytes 1572868
  83.2 5.5 %copy-start.4 = (f32[32,512]{1,0:T(8,128)S(1)}, f32[32,512]{1,0:T(8,128)}, u32[]{:S(2)}) copy-start(f32[32,512]{1,0:T(8,128)} %get-tuple-element.31) | copy-start | bytes 196612
  83.2 6.2 %copy-start.3 = (f32[32,512]{1,0:T(8,128)S(1)}, f32[32,512]{1,0:T(8,128)}, u32[]{:S(2)}) copy-start(f32[32,512]{1,0:T(8,128)} %get-tuple-element.32) | copy-start | bytes 196612
  83.2 6.8 %copy-start.2 = (f32[32,512]{1,0:T(8,128)S(1)}, f32[32,512]{1,0:T(8,128)}, u32[]{:S(2)}) copy-start(f32[32,512]{1,0:T(8,128)} %get-tuple-element.33) | copy-start | bytes 196612
  83.2 7.4 %copy-start.1 = (f32[3,32,512]{2,1,0:T(8,128)S(1)}, f32[3,32,512]{2,1,0:T(8,128)}, u32[]{:S(2)}) copy-start(f32[3,32,512]{2,1,0:T(8,128)} %get-tuple-element.34) | copy-start | bytes 589828

commit v2 on v1

v2 whole, which is shorter than its diff:
```python
import functools

import jax
import jax.numpy as jnp
from jax import lax
from jax.experimental import pallas as pl
from jax.experimental.pallas import tpu as pltpu
from jax.sharding import PartitionSpec as P

STEP = 100
F32 = jnp.float32
BF16 = jnp.bfloat16
MESH = pl.DeviceIdType.MESH
FIRST = "xxxxxxxx"
ORDER = (
    "prod0", "xa0", "xa1", "prod1", "xb0", "xa2", "ag1", "prod2", "xb1", "xa3", "y0", "agy0",
    "c0", "xb2", "xa4", "y1", "ag2", "agy1", "c1", "prod3", "xb3", "xa5", "y2", "z0", "c2",
    "xb4", "xa6", "y3", "z1", "ag3", "agy2", "c3", "xb5", "xa7", "y4", "z2", "c4", "xb6", "y5",
    "z3", "ag4", "agy3", "c5", "xb7", "y6", "z4", "c6", "c7", "y7", "z5", "agy4", "z6", "z7",
    "update", "c8", "c9", "c10", "c11", "c12", "c13", "c14", "c15", "final", "spread",
)


def dot(a, b, ca, cb):
    return lax.dot_general(a, b, (((ca,), (cb,)), ((), ())), preferred_element_type=F32)


def kernel(
    tok_h, kg_h, w_h, ma_h, mo_h, mt_h, live_v, buddy_s,
    keys_o, ig_o, nw_o, nm_o, n1_o, n2_o, held_o,
    tok, tokS, kg, kgs, W, back, keysf, rstd, dots, Q, XA, XB, YS, YR, ZS, ZR, GA,
    state,
    loc, tk_s, tk_r, kg_s, kg_r, xa_s, xa_r, xb_s, xb_r, ys_s, ys_r, zs_s, zs_r,
    az_s, az_r, ay_s, ay_r, sib_s, sib_r, ga_s, ga_r, gs_s, gs_r,
):
    f = lax.axis_index("fsdp")
    d = lax.axis_index("dom")
    z, ylo = lax.div(f, 2), lax.rem(f, 2)
    yhi, x, c = lax.div(d, 8), lax.rem(lax.div(d, 2), 4), lax.rem(d, 2)
    y = yhi * 2 + ylo
    o = 1 - c

    def dev(x, y, z, c):
        return (z * 2 + lax.rem(y, 2), lax.div(y, 2) * 8 + x * 2 + c)

    def xat(j):
        return lax.rem(x + j, 4)

    def yat(j):
        return lax.rem(y + j, 4)

    def zat(j):
        return lax.rem(z + j, 8)

    sibling = dev(x, y, z, o)

    def local(i, src, dst):
        return pltpu.make_async_copy(src, dst, loc.at[i])

    def remote(src, dst, s, r, to):
        return pltpu.make_async_remote_copy(
            src_ref=src, dst_ref=dst, send_sem=s, recv_sem=r, device_id=to, device_id_type=MESH
        )

    sent = []

    def go(copy):
        copy.start()
        sent.append(copy)

    barrier = pltpu.get_barrier_semaphore()
    partners = [sibling]
    partners += [dev(xat(i), y, z, c) for i in (1, 2, 3)]
    partners += [dev(xat(i), yat(2), z, c) for i in (0, 1, 2, 3)]
    partners += [dev(x, yat(i), z, c) for i in (1, 3)]
    partners += [dev(x, y, zat(i), cc) for i in range(1, 8) for cc in range(2)]
    for who in partners:
        pl.semaphore_signal(barrier, inc=1, device_id=who, device_id_type=MESH)

    loads = [
        local(0, w_h, W.at[f]),
        local(1, tok_h, tok),
        local(2, kg_h, kg),
        local(3, ma_h, state.at[0]),
        local(4, mo_h, state.at[1]),
        local(5, mt_h, state.at[2]),
    ]
    for i in (1, 2, 0, 3, 4, 5):
        loads[i].start()

    def z_offset(k, core):
        one = 1 - 2 * core
        return -one * k if k <= 4 else one * (k - 4)

    def piece(k, core, other):
        zz = lax.rem(z + z_offset(k, core) + 8, 8)
        return zz * 2 + (1 - ylo if other else ylo)

    onward = dev(x, y, lax.rem(z + 1 - 2 * c + 8, 8), c)
    backward = dev(x, y, lax.rem(z - 1 + 2 * c + 8, 8), c)

    def az(k):
        to = onward if k < 5 else backward
        before = (k - 1) if k != 5 else 0
        src = W.at[piece(before, c, False), c]
        return remote(src, src, az_s.at[k - 1], az_r.at[k - 1], to)

    def az_in(k):
        src = W.at[piece(k, c, False), c]
        return remote(src, src, az_s.at[k - 1], az_r.at[k - 1], onward)

    def ay(k, side):
        src = W.at[piece(k, c, False), c, side]
        return remote(src, src, ay_s.at[k, side], ay_r.at[k, side], dev(x, yat(1 if side == 0 else 3), z, c))

    def ay_in(k, side):
        src = W.at[piece(k, c, True), c, side]
        return remote(src, src, ay_s.at[k, side], ay_r.at[k, side], dev(x, yat(1), z, c))

    def sib(k, other):
        src = W.at[piece(k, c, other), c]
        i = k + 8 * other
        return remote(src, src, sib_s.at[i], sib_r.at[i], sibling)

    def sib_in(k, other):
        src = W.at[piece(k, o, other), o]
        i = k + 8 * other
        return remote(src, src, sib_s.at[i], sib_r.at[i], sibling)

    steps = {0: (0,), 1: (1, 5), 2: (2, 6), 3: (3, 7), 4: (4,)}

    def gather(s):
        for k in steps[s]:
            if s:
                az_in(k).wait_recv()
            if k == 0:
                go(az(1))
                go(az(5))
            elif k not in (4, 7):
                go(az(k + 1))
            go(ay(k, 0))
            go(ay(k, 1))
            if k:
                go(sib(k, False))

    def gather_y(s):
        for k in steps[s]:
            ay_in(k, 0).wait_recv()
            ay_in(k, 1).wait_recv()
            go(sib(k, True))

    def wide(column):
        return jnp.concatenate([column] * 4, axis=1)

    def folded(v):
        return (v[:, :128] + v[:, 128:256]) + (v[:, 256:384] + v[:, 384:])

    def block(i):
        return pl.ds(pl.multiple_of(i * 512, 512), 512)

    loads[1].wait()
    dots[...] = jnp.zeros_like(dots)

    @pl.loop(0, 16)
    def _(i):
        v = tok[:, block(i)].astype(F32)
        dots[...] += folded(v * v)

    mean_square = jnp.sum(dots[...], axis=1, keepdims=True) * (1.0 / 8192)
    rstd[...] = jnp.broadcast_to(lax.rsqrt(mean_square + 1e-05), rstd.shape)
    dots[...] = jnp.zeros_like(dots)
    keysf[...] = jnp.zeros_like(keysf)
    flags = live_v[...].astype(F32)
    rows = lax.broadcasted_iota(jnp.int32, flags.shape, 0)
    cols = lax.broadcasted_iota(jnp.int32, flags.shape, 1)
    alive = jnp.sum(jnp.where((rows == f) & (cols == d), flags, 0.0))
    loads[2].wait()
    kgs[c] = (kg[...].astype(F32) * (wide(rstd[...]) * alive)).astype(BF16)

    pl.semaphore_wait(barrier, len(partners))

    def tokens_out(g):
        src = tok.at[:, pl.ds(pl.multiple_of((4 * o + g) * 1024, 1024), 1024)]
        return remote(src, tokS.at[g], tk_s.at[g], tk_r.at[g], sibling)

    def kg_out(core):
        return remote(kgs.at[core], kgs.at[core], kg_s.at[0], kg_r.at[0], sibling)

    go(kg_out(c))
    for g in range(4):
        go(tokens_out(g))
    loads[0].wait()
    gather(0)

    def product(g):
        if g == 0:
            kg_out(o).wait_recv()
        tokens_out(g).wait_recv()

        @pl.loop(0, 2)
        def _(low):
            mine = tok[:, block((4 * c + g) * 2 + low)]
            theirs = tokS[g, :, block(low)]
            part = (dot(mine, kgs[c], 0, 0) + dot(theirs, kgs[o], 0, 0)).astype(BF16)
            for yy in range(2):
                for xx in range(4):
                    for h in range(2):
                        row = yy * 256 + xx * 64 + h * 32
                        n = 2 * g + h
                        if FIRST[n] == "x":
                            Q[n, xx, 2 * yy + low] = part[row : row + 32]
                        else:
                            Q[n, 2 * yy + low, xx] = part[row : row + 32]

    def at_a(n, j):
        return xat(j) if FIRST[n] == "x" else yat(j)

    def at_b(n, j):
        return yat(j) if FIRST[n] == "x" else xat(j)

    def to_a(n, j):
        return dev(xat(j), y, z, c) if FIRST[n] == "x" else dev(x, yat(j), z, c)

    def to_b(n, j):
        return dev(x, yat(j), z, c) if FIRST[n] == "x" else dev(xat(j), y, z, c)

    def xa(n, i):
        j, h, to = ((2, 0, 1), (1, 1, 1), (2, 1, 3), (3, 0, 3))[i]
        src = Q.at[n, at_a(n, j), pl.ds(2 * h, 2)]
        return remote(src, XA.at[n, i], xa_s.at[n, i], xa_r.at[n, i], to_a(n, to))

    def xb(n, i):
        j = (1, 3)[i]
        src = Q.at[n, at_a(n, j), pl.ds(2 * i, 2)]
        return remote(src, XB.at[n, i], xb_s.at[n, i], xb_r.at[n, i], to_a(n, j))

    def x_first(n):
        for i in (0, 2, 1, 3):
            go(xa(n, i))

    def x_second(n):
        for i, j in ((0, 1), (1, 3)):
            xa(n, 2 * i).wait_recv()
            at = at_a(n, j)
            for b in range(2):
                Q[n, at, 2 * i + b] = (
                    Q[n, at, 2 * i + b].astype(F32) + XA[n, 2 * i, b].astype(F32)
                ).astype(BF16)
            go(xb(n, i))

    def ysend(n, j):
        return remote(
            YS.at[n, at_b(n, j)], YR.at[n, j - 1], ys_s.at[n, j - 1], ys_r.at[n, j - 1], to_b(n, j)
        )

    def y_stage(n):
        here = at_a(n, 0)
        for h, i in ((0, 3), (1, 1)):
            xa(n, i).wait_recv()
            xb(n, h).wait_recv()
            for b in range(2):
                total = Q[n, here, 2 * h + b].astype(F32) + XA[n, i, b].astype(F32)
                YS[n, 2 * h + b] = (total + XB[n, h, b].astype(F32)).astype(BF16)
        for j in (2, 1, 3):
            go(ysend(n, j))

    def zsend(n):
        return remote(
            ZS.at[n], ZR.at[z], zs_s.at[n], zs_r.at[z], dev(x, y, 4 * c + n // 2, n % 2)
        )

    def kept(n):
        return (z == 4 * c + n // 2) & (c == n % 2)

    def z_stage(n):
        total = YS[n, at_b(n, 0)].astype(F32)
        for j in (1, 2, 3):
            ysend(n, j).wait_recv()
            total = total + YR[n, j - 1].astype(F32)

        @pl.when(kept(n))
        def _():
            ZR[z] = total.astype(BF16)

        @pl.when(jnp.logical_not(kept(n)))
        def _():
            ZS[n] = total.astype(BF16)
            zsend(n).start()

    chip = lax.div(d, 2)
    others = [(i, j) for j in (0, 2) for i in range(4) if i or j]

    def spread_out(n):
        i, j = others[n]
        return remote(GA.at[c, chip], GA.at[c, chip], ga_s.at[n], ga_r.at[n], dev(xat(i), yat(j), z, c))

    def source(n):
        i, j = others[n]
        return lax.div(yat(j), 2) * 4 + lax.rem(x - i + 4, 4)

    def spread_in(n):
        slot = GA.at[c, source(n)]
        return remote(slot, slot, ga_s.at[n], ga_r.at[n], sibling)

    def relay(n, core):
        slot = GA.at[core, source(n) if n < 7 else chip]
        return remote(slot, slot, gs_s.at[n], gs_r.at[n], sibling)

    def update():
        total = jnp.zeros((32, 512), F32)
        for j in range(1, 9):
            slot = zat(j)
            here = ZR.at[slot]
            if j < 8:
                remote(here, here, zs_s.at[0], zs_r.at[slot], sibling).wait_recv()
            else:

                @pl.when(c != lax.div(z, 4))
                def _():
                    remote(here, here, zs_s.at[0], zs_r.at[slot], sibling).wait_recv()

            total = total + ZR[slot].astype(F32)
        grad = total * (256.0 / (jnp.sum(live_v[...].astype(F32)) * 256.0))
        for copy in loads[3:]:
            copy.wait()
        one = 0.9 * state[1] + 0.1 * grad
        two = 0.95 * state[2] + 0.05 * grad * grad
        first = 1.0 - 0.9**STEP
        second = 1.0 - 0.95**STEP
        step = one / first / (jnp.sqrt(two / second) + 1e-08)
        master = state[0] - 0.002 * (step + 0.1 * state[0])
        for i, (v, ref) in enumerate(((master, nm_o), (one, n1_o), (two, n2_o))):
            ref[...] = v
            GA[c, chip, i] = v.astype(BF16)
        for n in range(7):
            go(spread_out(n))
        go(relay(7, c))

    def spread():
        for n in range(7):
            spread_in(n).wait_recv()
            go(relay(n, c))
        for n in range(8):
            relay(n, o).wait_recv()
        for core in range(2):
            nw_o[:, core] = GA[core, :, 0]
        src = jnp.int32(0)
        for s in range(16):
            src = jnp.where(buddy_s[s] == d, s, src)
        held_o[...] = GA[lax.rem(src, 2), lax.div(src, 2)].astype(F32)

    tasks = [(s, k, other) for s in range(5) for other in (False, True) for k in steps[s]]

    def compute(i):
        s, k, other = tasks[i]
        mirror = 0 if s == 0 else 4 if s == 4 else k + 4 if k < 4 else k - 4
        if k or other:
            sib_in(mirror, other).wait_recv()
        ff = piece(k, c, other)
        w = W[ff].reshape(512, 512)
        t = tok[:, block(ff)].astype(F32)
        keysf[...] += dot((t * wide(rstd[...])).astype(BF16), w, 1, 0)
        b = dot(kg[...], w, 1, 1)
        back[:, block(ff)] = b
        dots[...] += folded(b * t)

    def final():
        r = rstd[...]
        keys_o[...] = keysf[...].astype(BF16)
        mean = jnp.sum(dots[...], axis=1, keepdims=True) * (1.0 / 8192)
        dots[...] = r * r * r * mean

        @pl.loop(0, 16)
        def _(i):
            at = block(i)
            less = tok[:, at].astype(F32) * wide(dots[...])
            ig_o[:, at] = (wide(rstd[...]) * back[:, at] - less).astype(BF16)

    run = dict(update=update, spread=spread, final=final)
    for s in range(5):
        run[f"ag{s}"] = functools.partial(gather, s)
        run[f"agy{s}"] = functools.partial(gather_y, s)
    for i in range(16):
        run[f"c{i}"] = functools.partial(compute, i)
    for g in range(4):
        run[f"prod{g}"] = functools.partial(product, g)
    for n in range(8):
        run[f"xa{n}"] = functools.partial(x_first, n)
        run[f"xb{n}"] = functools.partial(x_second, n)
        run[f"y{n}"] = functools.partial(y_stage, n)
        run[f"z{n}"] = functools.partial(z_stage, n)
    for name in ORDER:
        run[name]()

    for copy in sent:
        copy.wait_send()
    for n in range(8):

        @pl.when(jnp.logical_not(kept(n)))
        def _():
            zsend(n).wait_send()


def hand_on(*refs):
    n = len(refs) // 2
    copies = [pltpu.make_async_copy(refs[i], refs[n + i], refs[-1].at[i]) for i in range(n)]
    for copy in copies:
        copy.start()
    for copy in copies:
        copy.wait()


def on_device(tokens, key_grad, weight, master, moment_one, moment_two, live, buddy):
    hbm = pl.BlockSpec(memory_space=pl.ANY)
    dma = pltpu.SemaphoreType.DMA
    out = jax.ShapeDtypeStruct
    vm = pltpu.VMEM
    shapes = (
        out((256, 512), BF16),
        out((256, 8192), BF16),
        out((8, 2, 32, 512), BF16),
        out((32, 512), F32),
        out((32, 512), F32),
        out((32, 512), F32),
        out((3, 32, 512), F32),
    )
    made = pl.pallas_call(
        kernel,
        out_shape=tuple(pltpu.VMEM(one.shape, one.dtype) for one in shapes),
        in_specs=[hbm] * 6
        + [pl.BlockSpec(memory_space=pltpu.VMEM), pl.BlockSpec(memory_space=pltpu.SMEM)],
        out_specs=(pl.BlockSpec(memory_space=pltpu.VMEM),) * 7,
        scratch_shapes=[
            vm((256, 8192), BF16),
            vm((4, 256, 1024), BF16),
            vm((256, 512), BF16),
            vm((2, 256, 512), BF16),
            vm((16, 2, 2, 128, 512), BF16),
            vm((256, 8192), F32),
            vm((256, 512), F32),
            vm((256, 128), F32),
            vm((256, 128), F32),
            vm((8, 4, 4, 32, 512), BF16),
            vm((8, 4, 2, 32, 512), BF16),
            vm((8, 2, 2, 32, 512), BF16),
            vm((8, 4, 32, 512), BF16),
            vm((8, 3, 32, 512), BF16),
            vm((8, 32, 512), BF16),
            vm((8, 32, 512), BF16),
            vm((2, 8, 3, 32, 512), BF16),
            vm((3, 32, 512), F32),
            dma((6,)),
            dma((4,)), dma((4,)),
            dma((1,)), dma((1,)),
            dma((8, 4)), dma((8, 4)),
            dma((8, 2)), dma((8, 2)),
            dma((8, 3)), dma((8, 3)),
            dma((8,)), dma((8,)),
            dma((7,)), dma((7,)),
            dma((8, 2)), dma((8, 2)),
            dma((16,)), dma((16,)),
            dma((7,)), dma((7,)),
            dma((8,)), dma((8,)),
        ],
        compiler_params=pltpu.CompilerParams(
            collective_id=0, has_side_effects=True, vmem_limit_bytes=58 << 20
        ),
        cost_estimate=pl.CostEstimate(flops=6 << 30, bytes_accessed=24 << 20, transcendentals=0),
    )(tokens, key_grad, weight.reshape(2, 2, 128, 512), master, moment_one, moment_two, live, buddy)
    made = [pltpu.with_memory_space_constraint(one, pltpu.VMEM) for one in made]
    keys, ig, nw, nm, n1, n2, held = pl.pallas_call(
        hand_on,
        out_shape=shapes,
        in_specs=[pl.BlockSpec(memory_space=pltpu.VMEM)] * 7,
        out_specs=(hbm,) * 7,
        scratch_shapes=[dma((7,))],
        compiler_params=pltpu.CompilerParams(vmem_limit_bytes=4 << 20),
    )(*made)
    return keys, ig, nw.reshape(512, 512), nm, n1, n2, held


def solution(mesh):
    both = P(("fsdp", "dom"), None)
    return jax.shard_map(
        on_device,
        mesh=mesh,
        in_specs=(both, both, P("fsdp", None), both, both, both, P(), P()),
        out_specs=(both, both, P("fsdp", None), both, both, both, P(None, ("fsdp", "dom"), None)),
        check_vma=False,
    )
```

time: 91.5 us -> 76.6 us (0.84)
  the two profiles are of different devices: /device:TPU:225 before, /device:TPU:97 now
where the time goes in v2:
time: 76.6 us; the launch traced here: 76.4 us
  Pallas kernels  75.8 us (99%)
    pallas_call x1, Pallas kernels, on_device(): pl.pallas_call(kernel, out_shape=tuple((pltpu.VMEM(one.shape, one.dtype)...  73.4 us
    pallas_call x1, Pallas kernels, on_device(): pl.pallas_call(hand_on, out_shape=shapes, in_specs=[pl.BlockSpec(memory_s...  2.43 us

profile of v2, /device:TPU:97, one launch (start us, length us, event | category | flops | bytes accessed | tf_op | source)
XLA Modules:
  0.0 76.4 jit_solution(5365498063659613021)
XLA Ops:
  0.6 73.4 %shard_map.135 = (bf16[256,512]{1,0:T(8,128)(2,1)S(1)}, bf16[256,8192]{1,0:T(8,128)(2,1)S(1)}, bf16[8,2,32,512]{3,2,1,0:T(8,128)(2,1)S(1)}, f32[32,512]{1,0:T(8,...) custom-call(bf16[256,8192]{1,0:T(8,128)(2,1)} %tok_h.1, bf16[256,512]{1,0:T(8,128)(2,1)} %kg_h.1, ...), custom_call_target="tpu_custom_call" | custom-call | flops 6442450944 | bytes 25165824 | tf_op jit(solution)/shard_map/pallas_call | solution.py:427
  74.0 2.4 %shard_map.136 = (bf16[256,512]{1,0:T(8,128)(2,1)}, bf16[256,8192]{1,0:T(8,128)(2,1)}, bf16[8,2,32,512]{3,2,1,0:T(8,128)(2,1)}, f32[32,512]{1,0:T(8,128)}, f32[3...) custom-call(bf16[256,512]{1,0:T(8,128)(2,1)S(1)} %get-tuple-element.21.refs_0_, ...), custom_call_target="tpu_custom_call" | custom-call | tf_op jit(solution)/shard_map/pallas_call | solution.py:471

commit v3 on v2

--- a/solution.py
+++ b/solution.py
@@ -11,7 +11,7 @@
 F32 = jnp.float32
 BF16 = jnp.bfloat16
 MESH = pl.DeviceIdType.MESH
-FIRST = "xxxxxxxx"
+FIRST = "yxxxxxxx"
 ORDER = (
     "prod0", "xa0", "xa1", "prod1", "xb0", "xa2", "ag1", "prod2", "xb1", "xa3", "y0", "agy0",
     "c0", "xb2", "xa4", "y1", "ag2", "agy1", "c1", "prod3", "xb3", "xa5", "y2", "z0", "c2",
@@ -68,6 +68,22 @@
         copy.start()
         sent.append(copy)
 
+    def quarter(i):
+        at = pl.ds(i * 2048, 2048)
+        return local(6 + i, tok_h.at[:, at], tok.at[:, at])
+
+    for i in range(4):
+        quarter(i).start()
+    loads = [
+        local(0, w_h, W.at[f]),
+        local(1, kg_h, kg),
+        local(2, ma_h, state.at[0]),
+        local(3, mo_h, state.at[1]),
+        local(4, mt_h, state.at[2]),
+    ]
+    for i in (1, 0, 2, 3, 4):
+        loads[i].start()
+
     barrier = pltpu.get_barrier_semaphore()
     partners = [sibling]
     partners += [dev(xat(i), y, z, c) for i in (1, 2, 3)]
@@ -76,17 +92,6 @@
     partners += [dev(x, y, zat(i), cc) for i in range(1, 8) for cc in range(2)]
     for who in partners:
         pl.semaphore_signal(barrier, inc=1, device_id=who, device_id_type=MESH)
-
-    loads = [
-        local(0, w_h, W.at[f]),
-        local(1, tok_h, tok),
-        local(2, kg_h, kg),
-        local(3, ma_h, state.at[0]),
-        local(4, mo_h, state.at[1]),
-        local(5, mt_h, state.at[2]),
-    ]
-    for i in (1, 2, 0, 3, 4, 5):
-        loads[i].start()
 
     def z_offset(k, core):
         one = 1 - 2 * core
@@ -158,13 +163,14 @@
     def block(i):
         return pl.ds(pl.multiple_of(i * 512, 512), 512)
 
-    loads[1].wait()
     dots[...] = jnp.zeros_like(dots)
-
-    @pl.loop(0, 16)
-    def _(i):
-        v = tok[:, block(i)].astype(F32)
-        dots[...] += folded(v * v)
+    for part in range(4):
+        quarter(part).wait()
+
+        @pl.loop(4 * part, 4 * part + 4)
+        def _(i):
+            v = tok[:, block(i)].astype(F32)
+            dots[...] += folded(v * v)
 
     mean_square = jnp.sum(dots[...], axis=1, keepdims=True) * (1.0 / 8192)
     rstd[...] = jnp.broadcast_to(lax.rsqrt(mean_square + 1e-05), rstd.shape)
@@ -174,7 +180,7 @@
     rows = lax.broadcasted_iota(jnp.int32, flags.shape, 0)
     cols = lax.broadcasted_iota(jnp.int32, flags.shape, 1)
     alive = jnp.sum(jnp.where((rows == f) & (cols == d), flags, 0.0))
-    loads[2].wait()
+    loads[1].wait()
     kgs[c] = (kg[...].astype(F32) * (wide(rstd[...]) * alive)).astype(BF16)
 
     pl.semaphore_wait(barrier, len(partners))
@@ -321,7 +327,7 @@
 
             total = total + ZR[slot].astype(F32)
         grad = total * (256.0 / (jnp.sum(live_v[...].astype(F32)) * 256.0))
-        for copy in loads[3:]:
+        for copy in loads[2:]:
             copy.wait()
         one = 0.9 * state[1] + 0.1 * grad
         two = 0.95 * state[2] + 0.05 * grad * grad
@@ -449,7 +455,7 @@
             vm((8, 32, 512), BF16),
             vm((2, 8, 3, 32, 512), BF16),
             vm((3, 32, 512), F32),
-            dma((6,)),
+            dma((10,)),
             dma((4,)), dma((4,)),
             dma((1,)), dma((1,)),
             dma((8, 4)), dma((8, 4)),

time: 76.6 us -> 75.5 us (0.986)
  Pallas kernels: 75.8 us -> 74.7 us
    pallas_call x1, Pallas kernels: 73.4 us -> 72.3 us  [on_device(): pl.pallas_call(kernel, out_shape=tuple((pltpu.VMEM(one.shape, one.dtype)...]
where the time goes in v3:
time: 75.5 us; the launch traced here: 75.4 us
  Pallas kernels  74.7 us (99%)
    pallas_call x1, Pallas kernels, on_device(): pl.pallas_call(kernel, out_shape=tuple((pltpu.VMEM(one.shape, one.dtype)...  72.3 us
    pallas_call x1, Pallas kernels, on_device(): pl.pallas_call(hand_on, out_shape=shapes, in_specs=[pl.BlockSpec(memory_s...  2.43 us

profile of v3, /device:TPU:97, one launch (start us, length us, event | category | flops | bytes accessed | tf_op | source)
XLA Modules:
  0.0 75.4 jit_solution(7460166356997314917)
XLA Ops:
  0.6 72.3 %shard_map.135 = (bf16[256,512]{1,0:T(8,128)(2,1)S(1)}, bf16[256,8192]{1,0:T(8,128)(2,1)S(1)}, bf16[8,2,32,512]{3,2,1,0:T(8,128)(2,1)S(1)}, f32[32,512]{1,0:T(8,...) custom-call(bf16[256,8192]{1,0:T(8,128)(2,1)} %tok_h.1, bf16[256,512]{1,0:T(8,128)(2,1)} %kg_h.1, ...), custom_call_target="tpu_custom_call" | custom-call | flops 6442450944 | bytes 25165824 | tf_op jit(solution)/shard_map/pallas_call | solution.py:433
  72.9 2.4 %shard_map.136 = (bf16[256,512]{1,0:T(8,128)(2,1)}, bf16[256,8192]{1,0:T(8,128)(2,1)}, bf16[8,2,32,512]{3,2,1,0:T(8,128)(2,1)}, f32[32,512]{1,0:T(8,128)}, f32[3...) custom-call(bf16[256,512]{1,0:T(8,128)(2,1)S(1)} %get-tuple-element.21.refs_0_, ...), custom_call_target="tpu_custom_call" | custom-call | tf_op jit(solution)/shard_map/pallas_call | solution.py:477
